TPU v7x, 512 devices: a whole 4x4x16 slice. The times are simulated.
512 devices in a mesh: blk: 128 (over x, z, core), gz: 4 (over y).
Axes of the slice: x: 4, y: 4, z: 16, core: 2. Of those that a mesh axis runs over, the one named last changes fastest.
Arguments:
- fixed: bfloat16 [128, 32, 32, 128], P('blk', 'gz'), may hold values from -6 to 6
- moving: bfloat16 [128, 32, 32, 128], P('blk', 'gz'), may hold values from -6 to 6
- block_place: int32 [128], P('blk'), may hold values from 0 to 127, each once
- tissue: int32 [128], P('blk'), may hold values 0 or 1
Outputs:
- velocity: float32 [3, 2, 32, 64], replicated
- cc_map: float32 [128, 32, 32, 128], P('blk', 'gz')
Inputs may be any that keep to these rules, and one draw needn't show every extreme that they name: `block_place`: each block position from 0 to 127 is named by exactly one block.
All inputs are finite; a program needn't handle non-finite values. No bound on the sum of `tissue` on one device may be relied on, other than what follows from the above.
Results may differ from a plain program's by a relative error of at most 0.0004.
Values may be sent and summed in bfloat16 or wider, within the bound.
A program may use at most 64 MiB of HBM per device.

v0:
```python
import math
import jax
import jax.numpy as jnp
from jax import lax
from jax.sharding import PartitionSpec as P

SCALE = 16
GY = 8
ITERS = 2
EXACT = lax.Precision.HIGHEST
EPSILON = 1e-05
STEP_LENGTH = 0.5
BOX_TAPS = [1.0 / 9.0] * 9
GAUSS_RAW = [math.exp(-((offset - 3) ** 2) / 4.5) for offset in range(7)]
GAUSS_TAPS = [value / sum(GAUSS_RAW) for value in GAUSS_RAW]


def with_halo(block, sides, width):
    for axis, dim in sides:
        count = lax.axis_size(axis)
        forward = [(i, i + 1) for i in range(count - 1)]
        backward = [(target, source) for source, target in forward]
        low = lax.ppermute(
            lax.slice_in_dim(block, block.shape[dim] - width, None, axis=dim), axis, forward
        )
        high = lax.ppermute(lax.slice_in_dim(block, 0, width, axis=dim), axis, backward)
        block = jnp.concatenate([low, block, high], axis=dim)
    return block


def tap_matrix(count, taps):
    radius = len(taps) // 2
    rows = jnp.arange(count)[:, None]
    cols = jnp.arange(count)[None, :]
    matrix = jnp.zeros((count, count), jnp.float32)
    for offset, weight in enumerate(taps):
        matrix = matrix + weight * (rows - cols == offset - radius).astype(jnp.float32)
    return matrix


def along_rows(field, matrix):
    return jnp.einsum("...xy,xu->...uy", field, matrix, precision=EXACT)


def along_cols(field, matrix):
    return jnp.einsum("...y,yv->...v", field, matrix, precision=EXACT)


def planes_filter(field, taps, count):
    total = jnp.zeros(field.shape[:-3] + (count,) + field.shape[-2:], jnp.float32)
    for offset, weight in enumerate(taps):
        total = total + weight * field[..., offset : offset + count, :, :]
    return total


def slope(field, axis):
    widths = [(0, 0)] * field.ndim
    widths[axis] = (1, 1)
    padded = jnp.pad(field, widths)
    length = field.shape[axis]
    upper = lax.slice_in_dim(padded, 2, length + 2, axis=axis)
    lower = lax.slice_in_dim(padded, 0, length, axis=axis)
    return 0.5 * (upper - lower)


def hat_rows(coords, count):
    where = jnp.clip((coords + 0.5) / SCALE - 0.5, 0.0, count - 1.0)
    marks = jnp.arange(count).astype(jnp.float32)
    return jnp.maximum(0.0, 1.0 - jnp.abs(where[..., None] - marks))


def statistics(means, fixed_c, warped_c):
    sii = means[2] - means[0] * means[0]
    sww = means[3] - means[1] * means[1]
    siw = means[4] - means[0] * means[1]
    denom = sii * sww + EPSILON
    similar = siw * siw / denom
    weight = (
        2.0 * siw / denom * (fixed_c - means[0] - siw / (sww + EPSILON) * (warped_c - means[1]))
    )
    return (similar, weight)


def smooth_axis(field, axis):
    widths = [(0, 0)] * field.ndim
    widths[axis] = (1, 1)
    padded = jnp.pad(field, widths)
    length = field.shape[axis]
    upper = lax.slice_in_dim(padded, 2, length + 2, axis=axis)
    lower = lax.slice_in_dim(padded, 0, length, axis=axis)
    return 0.25 * lower + 0.5 * field + 0.25 * upper


def regularize(velocity, total, coarse_rows, coarse_cols):
    block_rows = velocity.shape[2] // coarse_rows
    coarse_depth = velocity.shape[1]
    grid = total.reshape(block_rows, GY, 3, coarse_depth, coarse_rows, coarse_cols)
    grid = grid.transpose(2, 3, 0, 4, 1, 5).reshape(velocity.shape)
    regular = smooth_axis(smooth_axis(smooth_axis(grid, 1), 2), 3)
    return velocity + STEP_LENGTH * regular / jnp.sqrt(jnp.mean(regular * regular) + EPSILON)


def per_device(fixed, moving, block_place, tissue):
    slots, planes, row_side, col_side = fixed.shape
    depth_parts = lax.axis_size("gz")
    depth_index = lax.axis_index("gz")
    blocks = slots * lax.axis_size("blk")
    total_planes = planes * depth_parts
    coarse_depth = total_planes // SCALE
    coarse_rows = row_side // SCALE
    coarse_cols = col_side // SCALE
    grid_rows = blocks // GY * coarse_rows
    grid_cols = GY * coarse_cols
    stacked = jnp.stack([fixed, moving], 0)
    reach = 0
    haloed = with_halo(stacked, (("gz", 2),), 5)
    images = haloed.astype(jnp.float32)
    count_w = planes + 2 * (reach + 4)
    count_m = planes + 2 * reach
    fixed_w = images[0, :, 1 : 1 + count_w]
    moving_w = images[1, :, 1 : 1 + count_w]
    depth_slope = 0.5 * (images[1, :, 2 : 2 + count_w] - images[1, :, 0:count_w])
    row_slope = slope(moving_w, 2)
    col_slope = slope(moving_w, 3)
    depth_w = depth_index * planes - (reach + 4) + jnp.arange(count_w)
    inside_w = ((depth_w >= 0) & (depth_w < total_planes)).astype(jnp.float32)
    depth_hat = hat_rows(depth_w.astype(jnp.float32), coarse_depth)
    depth_m = depth_index * planes - reach + jnp.arange(count_m)
    inside_m = ((depth_m >= 0) & (depth_m < total_planes)).astype(jnp.float32)
    row_cells = jnp.arange(row_side)
    col_cells = jnp.arange(col_side)
    block_row = block_place // GY
    block_col = block_place % GY
    row_hat = hat_rows(
        (block_row[:, None] * row_side + row_cells[None, :]).astype(jnp.float32), grid_rows
    )
    col_hat = hat_rows(
        (block_col[:, None] * col_side + col_cells[None, :]).astype(jnp.float32), grid_cols
    )
    own_depth = depth_index * planes + jnp.arange(planes)
    restrict = (own_depth[None, :] // SCALE == jnp.arange(coarse_depth)[:, None]).astype(
        jnp.float32
    )
    box_rows = tap_matrix(row_side, BOX_TAPS)
    box_cols = tap_matrix(col_side, BOX_TAPS)
    gauss_rows = tap_matrix(row_side, GAUSS_TAPS)
    gauss_cols = tap_matrix(col_side, GAUSS_TAPS)
    tissue_scale = tissue.astype(jnp.float32)[:, None, None, None]
    positions = jnp.arange(blocks)
    velocity = jnp.zeros((3, coarse_depth, grid_rows, grid_cols), jnp.float32)
    correlation = jnp.zeros((slots, planes, row_side, col_side), jnp.float32)
    for rounds in range(ITERS):
        partial_value = jnp.einsum("ckab,sxa->sckxb", velocity, row_hat, precision=EXACT)
        partial_value = jnp.einsum("sckxb,syb->sckxy", partial_value, col_hat, precision=EXACT)
        shift = jnp.einsum("zk,sckxy->cszxy", depth_hat, partial_value, precision=EXACT)
        warped = moving_w + shift[0] * depth_slope + shift[1] * row_slope + shift[2] * col_slope
        warped = warped * inside_w[None, :, None, None]
        fields = jnp.stack(
            [fixed_w, warped, fixed_w * fixed_w, warped * warped, fixed_w * warped], 0
        )
        means = planes_filter(fields, BOX_TAPS, count_m)
        means = along_cols(along_rows(means, box_rows), box_cols)
        fixed_m = fixed_w[:, 4 : 4 + count_m]
        warped_m = warped[:, 4 : 4 + count_m]
        similar, weight = statistics(means, fixed_m, warped_m)
        scale = weight * tissue_scale * inside_m[None, :, None, None]
        depth_grad = 0.5 * (warped[:, 5 : 5 + count_m] - warped[:, 3 : 3 + count_m])
        force = jnp.stack(
            [scale * depth_grad, scale * slope(warped_m, 2), scale * slope(warped_m, 3)], 0
        )
        force = with_halo(force, (("gz", 2),), 3)
        smooth = planes_filter(force, GAUSS_TAPS, planes)
        smooth = along_cols(along_rows(smooth, gauss_rows), gauss_cols)
        local = smooth.reshape(3, slots, planes, coarse_rows, SCALE, coarse_cols, SCALE).sum(
            axis=(4, 6)
        )
        piece = jnp.einsum("kp,cspab->sckab", restrict, local, precision=EXACT).reshape(slots, -1)
        onehot_local = (positions[:, None] == block_place[None, :]).astype(jnp.float32)
        local_grid = jnp.dot(onehot_local, piece, precision=EXACT)
        total = lax.psum(local_grid, ("blk", "gz"))
        velocity = regularize(velocity, total, coarse_rows, coarse_cols)
        correlation = similar
    return (velocity, correlation)


def solution(mesh):
    return jax.shard_map(
        per_device,
        mesh=mesh,
        in_specs=(P("blk", "gz", None, None), P("blk", "gz", None, None), P("blk"), P("blk")),
        out_specs=(P(), P("blk", "gz", None, None)),
        check_vma=False,
    )
```

profile of v0, /device:TPU:1, one launch (start us, length us, event | category | flops | bytes accessed | tf_op | source)
XLA Modules:
  0.0 267.4 jit_solution(6952006898740505339)
XLA Ops:
  0.6 0.9 copy_bitcast_fusion
  1.6 4.0 %collective-permute-start = (bf16[2,1,5,32,128]{4,2,3,1,0:T(8,128)(2,1)S(1)}, bf16[2,1,5,32,128]{4,2,3,1,0:T(8,128)(2,1)S(1)}, u32[]{:S(2)}, u32[]{:S(2)}) collective-permute-start(bf16[2,1,5,32,128]{4,2,3,1,0:T(8,128)(2,1)S(1)} %get-tuple-element.38), channel_id=1, source_target_pairs={{0,1},{1,2},{2,3},{4,5},{5,6},{6,7},{8,9},{9,10},{10,11},{12,13},{... | collective-permute-start | bytes 245768 | tf_op jit(solution)/shard_map/ppermute | solution.py:23
  5.7 1.3 collective-permute-start.1
  9.3 0.9 fusion.94
  10.2 1.2 collective-permute-done.1
  12.1 0.5 fusion.3
  12.6 0.7 convolution_bitcast_fusion.2
  13.3 1.0 fusion.6
  14.7 3.5 %collective-permute-start.2 = (f32[3,1,3,32,128]{4,2,3,1,0:T(4,128)S(1)}, f32[3,1,3,32,128]{4,2,3,1,0:T(4,128)S(1)}, u32[]{:S(2)}, u32[]{:S(2)}) collective-permute-start(f32[3,1,3,32,128]{4,2,3,1,0:T(4,128)S(1)} %get-tuple-element.30), channel_id=1, source_target_pairs={{0,1},{1,2},{2,3},{4,5},{5,6},{6,7},{8,9},{9,10},{10,11},{12,13},{... | collective-permute-start | bytes 442376 | tf_op jit(solution)/shard_map/ppermute | solution.py:23
  18.2 1.3 collective-permute-start.3
  19.6 1.3 collective-permute-done.2
  20.8 3.8 %collective-permute-done.3 = f32[3,1,3,32,128]{4,2,3,1,0:T(4,128)S(1)} collective-permute-done((f32[3,1,3,32,128]{4,2,3,1,0:T(4,128)S(1)}, f32[3,1,3,32,128]{4,2,3,1,0:T(4,128)S(1)}, u32[]{:S(2)}, u32[]{:S(2)}) %collective-permute-start.3) | collective-permute-done | bytes 147488 | tf_op jit(solution)/shard_map/ppermute | solution.py:26
  25.1 0.5 fusion.26
  25.6 3.3 %convolution_reduce_fusion.1 = f32[3,8,2,8]{3,2,1,0:T(2,128)S(1)} fusion(f32[3,8,2,16,128,1]{4,3,5,2,1,0:T(8,128)S(1)} %bitcast.237, f32[8,16,128,1,1,1]{2,1,0,5,4,3:T(8,128)S(1)} %bitcast.238), kind=kOutput, calls=%fused_computation.1 | convolution fusion | flops 151092864 | bytes 460288 | tf_op jit(solution)/shard_map/...y,yv->...v/dot_general | solution.py:46
  29.7 1.2 copy.70
  31.0 1.4 reshape.690
  32.3 111.2 %psum.14 = f32[3,2,32,64]{3,2,1,0:T(8,128)S(1)} all-reduce(f32[3,2,32,64]{3,2,1,0:T(8,128)S(1)} %reshape.690), channel_id=1, replica_groups=mesh['blk'=128,'gz'=4] {'blk','gz'}, use_global_device_ids=true, to_apply=%region_1.2 | all-reduce | flops 12288 | bytes 98304 | tf_op jit(solution)/shard_map/psum | solution.py:180
  143.6 0.7 multiply_reduce_fusion.1
  145.8 0.9 convolution_bitcast_fusion
  147.0 0.5 fusion.1
  147.5 0.7 convolution_bitcast_fusion.1
  148.2 1.0 fusion.4
  149.7 1.4 collective-permute-start.4
  151.1 1.3 collective-permute-start.5
  152.4 0.7 copy.84
  153.1 1.5 collective-permute-done.4
  154.6 3.8 %collective-permute-done.5 = f32[3,1,3,32,128]{4,2,3,1,0:T(4,128)S(1)} collective-permute-done((f32[3,1,3,32,128]{4,2,3,1,0:T(4,128)S(1)}, f32[3,1,3,32,128]{4,2,3,1,0:T(4,128)S(1)}, u32[]{:S(2)}, u32[]{:S(2)}) %collective-permute-start.5) | collective-permute-done | bytes 147488 | tf_op jit(solution)/shard_map/ppermute | solution.py:26
  158.9 0.5 fusion.24
  159.3 3.3 %convolution_reduce_fusion = f32[3,8,2,8]{3,2,1,0:T(2,128)S(1)} fusion(f32[3,8,2,16,128,1]{4,3,5,2,1,0:T(8,128)S(1)} %bitcast.236, f32[8,16,128,1,1,1]{2,1,0,5,4,3:T(8,128)S(1)} %bitcast.239), kind=kOutput, calls=%fused_computation | convolution fusion | flops 151092864 | bytes 460288 | tf_op jit(solution)/shard_map/...y,yv->...v/dot_general | solution.py:46
  164.0 101.1 %psum.15 = f32[3,2,32,64]{3,2,1,0:T(8,128)S(1)} all-reduce(f32[3,2,32,64]{3,2,1,0:T(8,128)S(1)} %reshape.698), channel_id=1, replica_groups=mesh['blk'=128,'gz'=4] {'blk','gz'}, use_global_device_ids=true, to_apply=%region_4.5 | all-reduce | flops 12288 | bytes 98304 | tf_op jit(solution)/shard_map/psum | solution.py:180
  265.2 0.7 multiply_reduce_fusion
  266.6 0.8 divide_add_fusion
  (67 shorter events, 6.5 us)
Async XLA Ops:
  1.6 8.6 %collective-permute-start = (bf16[2,1,5,32,128]{4,2,3,1,0:T(8,128)(2,1)S(1)}, bf16[2,1,5,32,128]{4,2,3,1,0:T(8,128)(2,1)S(1)}, u32[]{:S(2)}, u32[]{:S(2)}) collective-permute-start(bf16[2,1,5,32,128]{4,2,3,1,0:T(8,128)(2,1)S(1)} %get-tuple-element.38), channel_id=1, source_target_pairs={{0,1},{1,2},{2,3},{4,5},{5,6},{6,7},{8,9},{9,10},{10,11},{12,13},{... | collective-permute-start | bytes 245768 | tf_op jit(solution)/shard_map/ppermute | solution.py:23
  5.7 5.7 %collective-permute-start.1 = (bf16[2,1,5,32,128]{4,2,3,1,0:T(8,128)(2,1)S(1)}, bf16[2,1,5,32,128]{4,2,3,1,0:T(8,128)(2,1)S(1)}, u32[]{:S(2)}, u32[]{:S(2)}) collective-permute-start(bf16[2,1,5,32,128]{4,2,3,1,0:T(8,128)(2,1)S(1)} %get-tuple-element.39), channel_id=1, source_target_pairs={{1,0},{2,1},{3,2},{5,4},{6,5},{7,6},{9,8},{10,9},{11,10},{13,12},{... | collective-permute-start | bytes 245768 | tf_op jit(solution)/shard_map/ppermute | solution.py:26
  7.6 2.6 copy-start
  7.8 2.4 copy-start.2
  14.7 6.1 %collective-permute-start.2 = (f32[3,1,3,32,128]{4,2,3,1,0:T(4,128)S(1)}, f32[3,1,3,32,128]{4,2,3,1,0:T(4,128)S(1)}, u32[]{:S(2)}, u32[]{:S(2)}) collective-permute-start(f32[3,1,3,32,128]{4,2,3,1,0:T(4,128)S(1)} %get-tuple-element.30), channel_id=1, source_target_pairs={{0,1},{1,2},{2,3},{4,5},{5,6},{6,7},{8,9},{9,10},{10,11},{12,13},{... | collective-permute-start | bytes 442376 | tf_op jit(solution)/shard_map/ppermute | solution.py:23
  18.2 6.4 %collective-permute-start.3 = (f32[3,1,3,32,128]{4,2,3,1,0:T(4,128)S(1)}, f32[3,1,3,32,128]{4,2,3,1,0:T(4,128)S(1)}, u32[]{:S(2)}, u32[]{:S(2)}) collective-permute-start(f32[3,1,3,32,128]{4,2,3,1,0:T(4,128)S(1)} %get-tuple-element.31), channel_id=1, source_target_pairs={{1,0},{2,1},{3,2},{5,4},{6,5},{7,6},{9,8},{10,9},{11,10},{13,12},{... | collective-permute-start | bytes 442376 | tf_op jit(solution)/shard_map/ppermute | solution.py:26
  29.7 115.3 %copy-start.1 = (f32[32]{0:T(128)S(1)}, f32[32]{0:T(128)}, u32[]{:S(2)}) copy-start(f32[32]{0:T(128)} %copy-done) | copy-start | bytes 388
  29.7 115.3 %copy-start.3 = (f32[32]{0:T(128)S(1)}, f32[32]{0:T(128)}, u32[]{:S(2)}) copy-start(f32[32]{0:T(128)} %copy-done.2) | copy-start | bytes 388
  149.7 4.9 %collective-permute-start.4 = (f32[3,1,3,32,128]{4,2,3,1,0:T(4,128)S(1)}, f32[3,1,3,32,128]{4,2,3,1,0:T(4,128)S(1)}, u32[]{:S(2)}, u32[]{:S(2)}) collective-permute-start(f32[3,1,3,32,128]{4,2,3,1,0:T(4,128)S(1)} %get-tuple-element.26), channel_id=1, source_target_pairs={{0,1},{1,2},{2,3},{4,5},{5,6},{6,7},{8,9},{9,10},{10,11},{12,13},{... | collective-permute-start | bytes 442376 | tf_op jit(solution)/shard_map/ppermute | solution.py:23
  151.1 7.3 %collective-permute-start.5 = (f32[3,1,3,32,128]{4,2,3,1,0:T(4,128)S(1)}, f32[3,1,3,32,128]{4,2,3,1,0:T(4,128)S(1)}, u32[]{:S(2)}, u32[]{:S(2)}) collective-permute-start(f32[3,1,3,32,128]{4,2,3,1,0:T(4,128)S(1)} %get-tuple-element.27), channel_id=1, source_target_pairs={{1,0},{2,1},{3,2},{5,4},{6,5},{7,6},{9,8},{10,9},{11,10},{13,12},{... | collective-permute-start | bytes 442376 | tf_op jit(solution)/shard_map/ppermute | solution.py:26
where the time goes:
time: 268 us; the launch traced here: 267 us
  blocking collectives  212 us (79%)
  matrix products  14.4 us (5%)
  starting transfers between devices  12.8 us (5%)
  waiting for transfers between devices  11.6 us (4%)
  local copies, waits for them, and re-layouts  6.26 us (2%)
  other arithmetic  6.11 us (2%)
  between operations  3.95 us (1%)
    psum x2, blocking collectives, per_device(): total = lax.psum(local_grid, ('blk', 'gz'))  212 us
    ppermute x3, starting transfers between devices, with_halo(): lax.ppermute(lax.slice_in_dim(block, block.shape[dim] - width, None, axis...  8.92 us
    ppermute x3, waiting for transfers between devices, with_halo(): lax.ppermute(lax.slice_in_dim(block, 0, width, axis=dim), axis, backward)  8.79 us
    dot_general x4, matrix products, along_cols(): return jnp.einsum('...y,yv->...v', field, matrix, precision=EXACT)  8.73 us
  transfers between devices with their start and end apart: 6, of which 5 were waited for; matrix products, arithmetic and copies ran while one was open for 1% of the time, Pallas kernels for 0%

commit v1 on v0

--- a/solution.py
+++ b/solution.py
@@ -177,7 +177,7 @@
         piece = jnp.einsum("kp,cspab->sckab", restrict, local, precision=EXACT).reshape(slots, -1)
         onehot_local = (positions[:, None] == block_place[None, :]).astype(jnp.float32)
         local_grid = jnp.dot(onehot_local, piece, precision=EXACT)
-        total = lax.psum(local_grid, ("blk", "gz"))
+        total = lax.psum(lax.psum(local_grid, "blk"), "gz")
         velocity = regularize(velocity, total, coarse_rows, coarse_cols)
         correlation = similar
     return (velocity, correlation)

time: 268 us -> 1080 us (4.03)
  blocking collectives: 212 us -> 1020 us
    psum x2 -> x4, blocking collectives: 212 us -> 1020 us  [per_device(): total = lax.psum(lax.psum(local_grid, 'blk'), 'gz')]
  transfers between devices with their start and end apart: 6 -> 6, of which waited for: 5 -> 5; matrix products, arithmetic and copies ran while one was open for 1% -> 0% of each run, Pallas kernels for 0% -> 0%
where the time goes in v1:
time: 1080 us; the launch traced here: 1070 us
  blocking collectives  1020 us (94%)
  matrix products  14.4 us (1%)
  starting transfers between devices  12.8 us (1%)
    psum x4, blocking collectives, per_device(): total = lax.psum(lax.psum(local_grid, 'blk'), 'gz')  1020 us
  transfers between devices with their start and end apart: 6, of which 5 were waited for; matrix products, arithmetic and copies ran while one was open for 0% of the time, Pallas kernels for 0%

profile of v1, /device:TPU:1, one launch (start us, length us, event | category | flops | bytes accessed | tf_op | source)
XLA Modules:
  0.0 1072.7 jit_solution(14382476051411386191)
XLA Ops:
  0.6 0.9 copy_bitcast_fusion
  1.6 4.0 collective-permute-start
  5.7 1.3 collective-permute-start.1
  9.3 0.9 fusion.94
  10.2 1.2 collective-permute-done.1
  12.1 0.5 fusion.3
  12.6 0.7 convolution_bitcast_fusion.2
  13.3 1.0 fusion.6
  14.7 3.5 collective-permute-start.2
  18.2 1.3 collective-permute-start.3
  19.6 1.3 collective-permute-done.2
  20.8 3.8 collective-permute-done.3
  25.6 3.3 convolution_reduce_fusion.1
  29.3 496.7 %psum.28 = f32[128,96]{0,1:T(8,128)S(1)} all-reduce(f32[128,96]{0,1:T(8,128)S(1)} %broadcast_multiply_fusion.1), channel_id=1, replica_groups=mesh['blk'=128,'gz'=4] {'blk'}, use_global_device_ids=true, to_apply=%region_1.2 | all-reduce | flops 12288 | bytes 98304 | tf_op jit(solution)/shard_map/psum | solution.py:180
  526.4 1.2 copy.70
  527.7 1.4 reshape.690
  529.0 12.7 %psum.29 = f32[3,2,32,64]{3,2,1,0:T(8,128)S(1)} all-reduce(f32[3,2,32,64]{3,2,1,0:T(8,128)S(1)} %reshape.690), channel_id=1, replica_groups=mesh['blk'=128,'gz'=4] {'gz'}, use_global_device_ids=true, to_apply=%region_2.3 | all-reduce | flops 12288 | bytes 98304 | tf_op jit(solution)/shard_map/psum | solution.py:180
  541.8 0.7 multiply_reduce_fusion.1
  543.9 0.9 convolution_bitcast_fusion
  545.2 0.5 fusion.1
  545.7 0.7 convolution_bitcast_fusion.1
  546.4 1.0 fusion.4
  547.9 1.4 collective-permute-start.4
  549.3 1.3 collective-permute-start.5
  550.6 0.7 copy.84
  551.3 0.6 collective-permute-done.4
  551.9 3.8 collective-permute-done.5
  556.7 3.3 convolution_reduce_fusion
  560.3 496.1 %psum.30 = f32[128,96]{0,1:T(8,128)S(1)} all-reduce(f32[128,96]{0,1:T(8,128)S(1)} %broadcast_multiply_fusion), channel_id=1, replica_groups=mesh['blk'=128,'gz'=4] {'blk'}, use_global_device_ids=true, to_apply=%region_5.6 | all-reduce | flops 12288 | bytes 98304 | tf_op jit(solution)/shard_map/psum | solution.py:180
  1057.4 13.0 %psum.31 = f32[3,2,32,64]{3,2,1,0:T(8,128)S(1)} all-reduce(f32[3,2,32,64]{3,2,1,0:T(8,128)S(1)} %reshape.698), channel_id=1, replica_groups=mesh['blk'=128,'gz'=4] {'gz'}, use_global_device_ids=true, to_apply=%region_6.7 | all-reduce | flops 12288 | bytes 98304 | tf_op jit(solution)/shard_map/psum | solution.py:180
  1070.6 0.7 multiply_reduce_fusion
  1072.0 0.8 divide_add_fusion
  (69 shorter events, 7.4 us)
Async XLA Ops:
  1.6 8.6 collective-permute-start
  5.7 5.7 collective-permute-start.1
  7.6 2.6 copy-start
  7.8 2.4 copy-start.2
  14.7 6.1 collective-permute-start.2
  18.2 6.4 collective-permute-start.3
  526.4 16.8 %copy-start.1 = (f32[32]{0:T(128)S(1)}, f32[32]{0:T(128)}, u32[]{:S(2)}) copy-start(f32[32]{0:T(128)} %copy-done) | copy-start | bytes 388
  526.4 16.8 %copy-start.3 = (f32[32]{0:T(128)S(1)}, f32[32]{0:T(128)}, u32[]{:S(2)}) copy-start(f32[32]{0:T(128)} %copy-done.2) | copy-start | bytes 388
  547.9 4.0 collective-permute-start.4
  549.3 6.4 collective-permute-start.5
